TPU v7x, 32 devices: a whole 2x2x4 slice. The times are simulated.
32 devices in a mesh: req: 16 (over z, x, core), ch: 2 (over y).
Axes of the slice: x: 2, y: 2, z: 4, core: 2. Of those that a mesh axis runs over, the one named last changes fastest.
Arguments:
- tokens: bfloat16 [32, 4096], P('req', 'ch'), may hold values from -80 to 80
- attn_gain: float32 [4096], P('ch'), may hold values from 0.1 to 1.9
- w_query: bfloat16 [4096, 4096], P('ch', 'req'), may hold values from -0.09375 to 0.09375
- w_keyval: bfloat16 [4096, 512], P('ch', 'req'), may hold values from -0.09375 to 0.09375
- cache: bfloat16 [2, 32, 256, 2048], P(None, 'req', 'ch'), may hold values from -70 to 70
- lengths: int32 [32], P('req'), may hold values from 1 to 2047, as said below
- write_pos: int32 [32], P('req'), may hold values from 0 to 2047
- w_out: bfloat16 [4096, 4096], P('ch', 'req'), may hold values from -0.09375 to 0.09375
- mlp_gain: float32 [4096], P('ch'), may hold values from 0.1 to 1.9
- w_gate_up: bfloat16 [4096, 24576], P('ch', 'req'), may hold values from -0.09375 to 0.09375
- w_down: bfloat16 [12288, 4096], P('req', 'ch'), may hold values from -0.0546875 to 0.0546875
Outputs:
- layer_out: bfloat16 [32, 4096], P('req', 'ch')
- kv_new: bfloat16 [32, 512], P('req', 'ch')
Inputs may be any that keep to these rules, and one draw needn't show every extreme that they name: lengths[b] earlier tokens of request b are in the cache; the largest equals 2047 in every draw. The new token of request b goes to slot write_pos[b]; its earlier tokens fill the slots before it, going back cyclically.
All inputs are finite; a program needn't handle non-finite values.
Results may differ from a plain program's by a relative error of at most 0.0064.
Values may be sent and summed in bfloat16 or wider, within the bound.
A program may use at most 64 MiB of HBM per device.

v0:
```python
import math

import jax
import jax.numpy as jnp
from jax import lax
from jax.sharding import PartitionSpec as P

D = 4096
H = 16
HD = 256


EPSILON = 1e-06


def rms_norm(values, gain):
    wide = values.astype(jnp.float32)
    squares = jnp.sum(wide * wide, axis=1)
    summed = lax.psum(squares, "ch")
    meansq = summed / D
    return (wide * lax.rsqrt(meansq + EPSILON)[:, None] * gain[None, :]).astype(jnp.bfloat16)


def body(
    tokens,
    attn_gain,
    w_query,
    w_keyval,
    cache,
    lengths,
    write_pos,
    w_out,
    mlp_gain,
    w_gate_up,
    w_down,
):
    rows = tokens.shape[0]
    chan = cache.shape[2]
    window = cache.shape[3]
    factor = 1.0 / math.sqrt(HD)
    normed = rms_norm(tokens, attn_gain)
    joined = jnp.concatenate([w_query, w_keyval], axis=1)
    head_parts = jnp.dot(
        lax.all_gather(normed, "req", axis=0, tiled=True),
        joined,
        preferred_element_type=jnp.float32,
    )
    query_cols = w_query.shape[1]
    query_part, keyval_part = (
        lax.all_to_all(head_parts[:, :query_cols], "req", split_axis=0, concat_axis=1, tiled=True),
        lax.all_to_all(head_parts[:, query_cols:], "req", split_axis=0, concat_axis=1, tiled=True),
    )
    query_sum, keyval_sum = (
        lax.psum_scatter(query_part, "ch", scatter_dimension=1, tiled=True),
        lax.psum_scatter(keyval_part, "ch", scatter_dimension=1, tiled=True),
    )
    queries = query_sum.astype(jnp.bfloat16).reshape(rows, H, chan)
    keyval_new = keyval_sum.astype(jnp.bfloat16)
    key_new = keyval_new[:, :chan]
    value_new = keyval_new[:, chan:]
    keys = cache[0]
    values_cache = cache[1]
    own_part = jnp.sum(
        queries.astype(jnp.float32) * key_new.astype(jnp.float32)[:, None, :], axis=-1
    )
    score_part = jnp.einsum("bhe,bew->bhw", queries, keys, preferred_element_type=jnp.float32)
    summed, own_sum = lax.psum((score_part, own_part), "ch")
    slot_index = jnp.arange(window, dtype=jnp.int32)
    offset = (write_pos[:, None] - 1 - slot_index[None, :]) % window
    usable = offset < lengths[:, None]
    scores = jnp.where(usable[:, None, :], summed * factor, -jnp.inf)
    own_score = own_sum * factor
    top = jnp.maximum(jnp.max(scores, axis=-1), own_score)
    weights = jnp.exp(scores - top[..., None])
    own_weight = jnp.exp(own_score - top)
    total = jnp.sum(weights, axis=-1) + own_weight
    weights_low = weights.astype(jnp.bfloat16)
    numer = jnp.einsum(
        "bhw,bew->bhe", weights_low, values_cache, preferred_element_type=jnp.float32
    )
    numer = (
        numer
        + own_weight.astype(jnp.bfloat16).astype(jnp.float32)[..., None]
        * value_new.astype(jnp.float32)[:, None, :]
    )
    attn_local = (numer / total[..., None]).astype(jnp.bfloat16).reshape(rows, H * chan)
    out_parts = jnp.dot(
        lax.all_gather(attn_local, "req", axis=0, tiled=True),
        w_out,
        preferred_element_type=jnp.float32,
    )
    out_part = lax.all_to_all(out_parts, "req", split_axis=0, concat_axis=1, tiled=True)
    out_sum = lax.psum_scatter(out_part, "ch", scatter_dimension=1, tiled=True)
    first = (tokens.astype(jnp.float32) + out_sum).astype(jnp.bfloat16)
    normed_two = rms_norm(first, mlp_gain)
    hidden_cols = w_gate_up.shape[1] // 2
    ffn_parts = jnp.dot(
        lax.all_gather(normed_two, "req", axis=0, tiled=True),
        w_gate_up,
        preferred_element_type=jnp.float32,
    )
    ffn_total = lax.psum(ffn_parts, "ch")
    hidden = (
        jax.nn.gelu(ffn_total[:, :hidden_cols], approximate=True) * ffn_total[:, hidden_cols:]
    ).astype(jnp.bfloat16)
    down_sum = lax.psum_scatter(
        jnp.dot(hidden, w_down, preferred_element_type=jnp.float32),
        "req",
        scatter_dimension=0,
        tiled=True,
    )
    layer_out = (first.astype(jnp.float32) + down_sum).astype(jnp.bfloat16)
    return (layer_out, keyval_new)


def solution(mesh):
    placed = (
        P("req", "ch"),
        P("ch"),
        P("ch", "req"),
        P("ch", "req"),
        P(None, "req", "ch", None),
        P("req"),
        P("req"),
        P("ch", "req"),
        P("ch"),
        P("ch", "req"),
        P("req", "ch"),
    )
    return jax.shard_map(
        body,
        mesh=mesh,
        in_specs=placed,
        out_specs=(P("req", "ch"), P("req", "ch")),
        check_vma=False,
    )
```

profile of v0, /device:TPU:1, one launch (start us, length us, event | category | flops | bytes accessed | tf_op | source)
XLA Modules:
  0.0 351.6 jit_solution(13919590285201111029)
XLA Ops:
  8.2 4.4 %psum.35 = f32[2]{0:T(128)S(1)} all-reduce(f32[2]{0:T(128)S(1)} %fusion.34), channel_id=1, replica_groups=mesh['req'=16,'ch'=2] {'ch'}, use_global_device_ids=true, to_apply=%region_1.0 | all-reduce | flops 2 | bytes 16 | tf_op jit(solution)/shard_map/psum | solution.py:19
  13.4 23.9 %all-gather = bf16[16,2,2048]{2,1,0:T(2,128)(2,1)S(1)} all-gather(bf16[1,2,2048]{2,1,0:T(2,128)(2,1)S(1)} %fusion.46), channel_id=1, replica_groups=mesh['req'=16,'ch'=2] {'req'}, dimensions={0}, use_global_device_ids=true | all-gather | bytes 139264 | tf_op jit(solution)/shard_map/all_gather | solution.py:44
  37.3 1.9 copy.15
  41.5 3.4 all-to-all-start.1
  45.6 5.3 %all-to-all-done.1 = f32[16,2,32]{2,1,0:T(2,128)S(1)} async-done(((f32[16,2,32]{2,1,0:T(2,128)}), f32[16,2,32]{2,1,0:T(2,128)S(1)}, u32[]{:S(2)}, u32[]{:S(2)}) %all-to-all-start.1) | async-done | bytes 4128 | tf_op jit(solution)/shard_map/all_to_all | solution.py:51
  50.9 4.0 %all-to-all-start = ((f32[16,2,256]{2,1,0:T(2,128)}), f32[16,2,256]{2,1,0:T(2,128)S(1)}, u32[]{:S(2)}, u32[]{:S(2)}) async-start(f32[16,2,256]{2,1,0:T(2,128)} %all_to_all.42), calls=%async_computation | async-start | bytes 65536 | tf_op jit(solution)/shard_map/all_to_all | solution.py:50
  55.9 5.0 %all-to-all-done = f32[16,2,256]{2,1,0:T(2,128)S(1)} async-done(((f32[16,2,256]{2,1,0:T(2,128)}), f32[16,2,256]{2,1,0:T(2,128)S(1)}, u32[]{:S(2)}, u32[]{:S(2)}) %all-to-all-start) | async-done | bytes 32800 | tf_op jit(solution)/shard_map/all_to_all | solution.py:50
  60.9 2.0 copy.17
  63.1 7.4 %reduce-scatter.12.cloned.1.call-done = f32[256,2]{1,0:T(8,128)} async-done(((f32[512,2]{1,0:T(8,128)}), f32[256,2]{1,0:T(8,128)}) %reduce-scatter.12.cloned.1.call-update) | async-done | bytes 2064
  71.5 33.2 %reduce-scatter.10.cloned.1.call-done = f32[2048,2]{1,0:T(8,128)} async-done(((f32[4096,2]{1,0:T(8,128)}), f32[2048,2]{1,0:T(8,128)}) %reduce-scatter.10.cloned.1.call-update) | async-done | bytes 16400
  106.3 2.2 fusion.7
  108.6 3.8 %psum.37 = f32[2,16]{1,0:T(2,128)S(1)} all-reduce(f32[2,16]{1,0:T(2,128)S(1)} %multiply_reduce_fusion), channel_id=1, replica_groups=mesh['req'=16,'ch'=2] {'ch'}, use_global_device_ids=true, to_apply=%region_7.8 | all-reduce | flops 32 | bytes 256 | tf_op jit(solution)/shard_map/psum | solution.py:67
  112.4 19.0 %all-reduce.5.cloned.1.call-done = f32[2,16,2048]{2,1,0:T(8,128)} async-done(((f32[2,16,2048]{2,1,0:T(8,128)}), f32[2,16,2048]{2,1,0:T(8,128)}) %all-reduce.5.cloned.1.call-update) | async-done | bytes 262160 | tf_op jit(solution)/shard_map/psum | solution.py:67
  133.6 1.7 fusion.5
  135.4 22.6 %all-gather.1 = bf16[16,2,2048]{2,1,0:T(2,128)(2,1)S(1)} all-gather(bf16[1,2,2048]{2,1,0:T(2,128)(2,1)S(1)} %reshape.73), channel_id=1, replica_groups=mesh['req'=16,'ch'=2] {'req'}, dimensions={0}, use_global_device_ids=true | all-gather | bytes 139264 | tf_op jit(solution)/shard_map/all_gather | solution.py:88
  159.7 8.5 %all_to_all.57 = f32[16,2,256]{2,1,0:T(2,128)S(1)} all-to-all(f32[16,2,256]{2,1,0:T(2,128)S(1)} %all_to_all.50), channel_id=1, replica_groups=mesh['req'=16,'ch'=2] {'req'}, dimensions={0} | all-to-all | bytes 65536 | tf_op jit(solution)/shard_map/all_to_all | solution.py:92
  168.2 2.0 copy.21
  170.3 28.4 %reduce-scatter.14.cloned.1.call-done = f32[2048,2]{1,0:T(8,128)} async-done(((f32[4096,2]{1,0:T(8,128)}), f32[2048,2]{1,0:T(8,128)}) %reduce-scatter.14.cloned.1.call-update) | async-done | bytes 16400
  200.4 3.8 %psum.38 = f32[2]{0:T(128)S(1)} all-reduce(f32[2]{0:T(128)S(1)} %get-tuple-element.2), channel_id=1, replica_groups=mesh['req'=16,'ch'=2] {'ch'}, use_global_device_ids=true, to_apply=%region_11.12 | all-reduce | flops 2 | bytes 16 | tf_op jit(solution)/shard_map/psum | solution.py:19
  204.3 23.3 %all-gather.2 = bf16[16,2,2048]{2,1,0:T(2,128)(2,1)S(1)} all-gather(bf16[1,2,2048]{2,1,0:T(2,128)(2,1)S(1)} %fusion.45), channel_id=1, replica_groups=mesh['req'=16,'ch'=2] {'req'}, dimensions={0}, use_global_device_ids=true | all-gather | bytes 139264 | tf_op jit(solution)/shard_map/all_gather | solution.py:98
  227.7 4.6 %fusion.58 = f32[32,1536]{1,0:T(8,128)} fusion(bf16[32,2048]{1,0:T(8,128)(2,1)S(1)} %reshape.76, bf16[2048,1536]{1,0:T(8,128)(2,1)} %param.20), kind=kOutput, calls=%fused_computation.78 | convolution fusion | flops 201326592 | bytes 6619136 | tf_op jit(solution)/shard_map/dot_general | solution.py:97
  232.4 17.8 %all-reduce.7.cloned.1.call-done = f32[32,1536]{1,0:T(8,128)} async-done(((f32[32,1536]{1,0:T(8,128)}), f32[32,1536]{1,0:T(8,128)}) %all-reduce.7.cloned.1.call-update) | async-done | bytes 196624 | tf_op jit(solution)/shard_map/psum | solution.py:102
  250.2 2.3 fusion.28
  253.7 89.6 %all-reduce.9.cloned.1.call-done = f32[32,2048]{1,0:T(8,128)} async-done(((f32[32,2048]{1,0:T(8,128)}), f32[32,2048]{1,0:T(8,128)}) %all-reduce.9.cloned.1.call-update) | async-done | bytes 262160
  (56 shorter events, 16.5 us)
Async XLA Ops:
  7.2 243.0 %copy-start = (bf16[768,2048]{1,0:T(8,128)(2,1)S(1)}, bf16[768,2048]{1,0:T(8,128)(2,1)}, u32[]{:S(2)}) copy-start(bf16[768,2048]{1,0:T(8,128)(2,1)} %param.21) | copy-start | bytes 9437188
  7.2 48.7 %copy-start.5 = (s32[2]{0:T(128)S(1)}, s32[2]{0:T(128)}, u32[]{:S(2)}) copy-start(s32[2]{0:T(128)} %param.17) | copy-start | bytes 28
  40.9 22.1 %copy-start.4 = (s32[2]{0:T(128)S(1)}, s32[2]{0:T(128)}, u32[]{:S(2)}) copy-start(s32[2]{0:T(128)} %param.16) | copy-start | bytes 28
  41.5 9.3 %all-to-all-start.1 = ((f32[16,2,32]{2,1,0:T(2,128)}), f32[16,2,32]{2,1,0:T(2,128)S(1)}, u32[]{:S(2)}, u32[]{:S(2)}) async-start(f32[16,2,32]{2,1,0:T(2,128)} %bitcast.4), calls=%async_computation.1 | async-start | bytes 32768 | tf_op jit(solution)/shard_map/all_to_all | solution.py:51
  50.9 10.0 %all-to-all-start = ((f32[16,2,256]{2,1,0:T(2,128)}), f32[16,2,256]{2,1,0:T(2,128)S(1)}, u32[]{:S(2)}, u32[]{:S(2)}) async-start(f32[16,2,256]{2,1,0:T(2,128)} %all_to_all.42), calls=%async_computation | async-start | bytes 65536 | tf_op jit(solution)/shard_map/all_to_all | solution.py:50
  54.9 15.6 %reduce-scatter.12.cloned.1.call-start = ((), (), s32[]{:S(2)}) async-start(), calls=%async_computation.9 | async-start | bytes 393216
  55.9 48.9 %reduce-scatter.10.cloned.1.call-start = ((), (), s32[]{:S(2)}) async-start(), calls=%async_computation.8 | async-start | bytes 3145728
  62.9 68.5 %all-reduce.5.cloned.1.call-start = ((), (), s32[]{:S(2)}) async-start(), calls=%async_computation.6 | async-start | bytes 524288 | tf_op jit(solution)/shard_map/psum | solution.py:67
  71.5 88.2 %copy-start.3 = (bf16[2,256]{1,0:T(2,128)(2,1)}, bf16[2,256]{1,0:T(2,128)(2,1)S(1)}, u32[]{:S(2)}) copy-start(bf16[2,256]{1,0:T(2,128)(2,1)S(1)} %copy.20) | copy-start | bytes 3076
  108.5 90.2 %reduce-scatter.14.cloned.1.call-start = ((), (), s32[]{:S(2)}) async-start(), calls=%async_computation.10 | async-start | bytes 3145728
  158.1 42.2 %copy-start.1 = (bf16[2,2048]{1,0:T(2,128)(2,1)S(1)}, bf16[2,2048]{1,0:T(2,128)(2,1)}, u32[]{:S(2)}) copy-start(bf16[2,2048]{1,0:T(2,128)(2,1)} %param.11) | copy-start | bytes 24580
  158.1 46.1 %copy-start.2 = (f32[2048]{0:T(1024)S(1)}, f32[2048]{0:T(1024)}, u32[]{:S(2)}) copy-start(f32[2048]{0:T(1024)} %param.19) | copy-start | bytes 24580
  170.3 79.9 %all-reduce.7.cloned.1.call-start = ((), (), s32[]{:S(2)}) async-start(), calls=%async_computation.7 | async-start | bytes 393216 | tf_op jit(solution)/shard_map/psum | solution.py:102
  232.3 20.2 %copy-start.6 = (u32[32]{0:T(128)S(1)}, u32[32]{0:T(128)}, u32[]{:S(2)}) copy-start(u32[32]{0:T(128)} %constant.45) | copy-start | bytes 388
  232.3 111.0 %all-reduce.9.cloned.1.call-start = ((), (), s32[]{:S(2)}) async-start(), calls=%async_computation.11 | async-start | bytes 524288
Sparse Core Ops, SparseCore 0:
  58.0 12.5 reduce-scatter.11
  72.8 31.8 reduce-scatter.9
  108.6 22.7 all-reduce.4
  170.4 28.2 reduce-scatter.13
  232.4 17.6 all-reduce.6
  253.4 89.8 all-reduce.8
where the time goes:
time: 352 us
  waiting for transfers between devices  206 us (59%)
  blocking collectives  90.3 us (26%)
  between operations  14.9 us (4%)
  matrix products  14 us (4%)
  local copies, waits for them, and re-layouts  13 us (4%)
  starting transfers between devices  7.71 us (2%)
  other arithmetic  5.9 us (2%)
    unnamed x10, waiting for transfers between devices  159 us
    all_gather x1, blocking collectives, body(): lax.all_gather(normed, 'req', axis=0, tiled=True)  23.9 us
    all_gather x1, blocking collectives, body(): lax.all_gather(normed_two, 'req', axis=0, tiled=True)  23.3 us
    all_gather x1, blocking collectives, body(): lax.all_gather(attn_local, 'req', axis=0, tiled=True)  22.6 us
    psum x1, waiting for transfers between devices, body(): summed, own_sum = lax.psum((score_part, own_part), 'ch')  19 us
    psum x1, waiting for transfers between devices, body(): ffn_total = lax.psum(ffn_parts, 'ch')  17.8 us
    unnamed x26, local copies, waits for them, and re-layouts  11.7 us
    all_to_all x1, blocking collectives, body(): lax.all_to_all(out_parts, 'req', split_axis=0, concat_axis=1, tiled=True)  8.55 us
  transfers between devices with their start and end apart: 8, of which 8 were waited for; matrix products, arithmetic and copies ran while one was open for 1% of the time, Pallas kernels for 0%

commit v1 on v0

--- a/solution.py
+++ b/solution.py
@@ -3,6 +3,8 @@
 import jax
 import jax.numpy as jnp
 from jax import lax
+from jax.experimental import pallas as pl
+from jax.experimental.pallas import tpu as pltpu
 from jax.sharding import PartitionSpec as P
 
 D = 4096
@@ -113,6 +115,529 @@
     return (layer_out, keyval_new)
 
 
+REQ = 16
+CH = 2
+ROWS = 2
+LANES = 128
+CHUNKS = 16
+HALF = REQ // CH
+BLOCK = ROWS * CHUNKS
+TILE = 8
+MESH = pl.DeviceIdType.MESH
+
+
+def place(chunk):
+    return (chunk % 2) * HALF + chunk // 2
+
+
+def fused_kernel(
+    tokens_ref,
+    attn_gain_ref,
+    w_query_hbm,
+    w_keyval_hbm,
+    cache_hbm,
+    lengths_ref,
+    write_pos_ref,
+    w_out_hbm,
+    mlp_gain_ref,
+    w_gate_up_hbm,
+    w_down_hbm,
+    out_ref,
+    kv_ref,
+    w_query,
+    w_keyval,
+    keys,
+    values,
+    w_out,
+    w_gate_up,
+    w_down,
+    own_block,
+    sends,
+    gathered,
+    wide,
+    parts_out,
+    parts_in,
+    score_out,
+    score_in,
+    own_out,
+    own_in,
+    square_out,
+    square_in,
+    ffn_own,
+    ffn_out,
+    ffn_in,
+    down_wide,
+    down_out,
+    down_in,
+    result,
+    load_sem,
+    gather_send,
+    gather_recv,
+    parts_send,
+    parts_recv,
+    score_send,
+    score_recv,
+    own_send,
+    own_recv,
+    square_send,
+    square_recv,
+    ffn_send,
+    ffn_recv,
+    down_send,
+    down_recv,
+):
+    req = lax.axis_index("req")
+    ch = lax.axis_index("ch")
+    other = 1 - ch
+    window = keys.shape[2]
+    hidden_cols = w_down.shape[0]
+    factor = 1.0 / math.sqrt(HD)
+    f32 = jnp.float32
+    bf16 = jnp.bfloat16
+
+    barrier = pltpu.get_barrier_semaphore()
+    me = req * CH + ch
+
+    def greet(step, carry):
+        peer = (me + step) % (REQ * CH)
+        pl.semaphore_signal(barrier, inc=1, device_id=(peer // CH, peer % CH), device_id_type=MESH)
+        return carry
+
+    lax.fori_loop(1, REQ * CH, greet, 0)
+
+    loads = [
+        pltpu.make_async_copy(src, dst, load_sem.at[index])
+        for index, (src, dst) in enumerate(
+            (
+                (w_query_hbm, w_query),
+                (w_keyval_hbm, w_keyval),
+                (cache_hbm.at[0], keys),
+                (cache_hbm.at[1], values),
+                (w_out_hbm, w_out),
+                (w_gate_up_hbm, w_gate_up),
+                (w_down_hbm, w_down),
+            )
+        )
+    ]
+    for load in loads:
+        load.start()
+
+    tokens = tokens_ref[...].astype(f32)
+    for row in range(ROWS):
+        for chunk in range(CHUNKS):
+            spot = row * CHUNKS + place(chunk)
+            own_block[spot : spot + 1, :] = tokens[row : row + 1, chunk * LANES : (chunk + 1) * LANES]
+
+    pl.semaphore_wait(barrier, REQ * CH - 1)
+
+    def block_of(index):
+        return pl.ds(pl.multiple_of(index * BLOCK, BLOCK), BLOCK)
+
+    def tile_of(index):
+        return pl.ds(pl.multiple_of(index * TILE, TILE), TILE)
+
+    def gather_copy(phase, peer, slot):
+        return pltpu.make_async_remote_copy(
+            src_ref=sends.at[phase],
+            dst_ref=gathered.at[phase, block_of(slot)],
+            send_sem=gather_send.at[phase, peer],
+            recv_sem=gather_recv.at[phase, slot],
+            device_id=(peer, ch),
+            device_id_type=MESH,
+        )
+
+    def gather(phase, block):
+        sends[phase] = block
+        gathered[phase, block_of(req), :] = block
+
+        def start(step, carry):
+            peer = (req + step) % REQ
+            gather_copy(phase, peer, req).start()
+            return carry
+
+        lax.fori_loop(1, REQ, start, 0)
+
+    def gather_wait(phase):
+        def wait(step, carry):
+            peer = (req + REQ - step) % REQ
+            gather_copy(phase, peer, peer).wait_recv()
+            return carry
+
+        lax.fori_loop(1, REQ, wait, 0)
+        wide[phase] = gathered[phase].astype(f32)
+
+    def chunk_rows(phase, chunk):
+        spot = place(chunk)
+        return jnp.concatenate(
+            [wide[phase, pl.ds(row * CHUNKS + spot, REQ, stride=BLOCK), :] for row in range(ROWS)],
+            axis=0,
+        )
+
+    def gained(phase, gain_ref):
+        total = None
+        pieces = []
+        for chunk in range(CHUNKS):
+            piece = chunk_rows(phase, chunk)
+            square = piece * piece
+            total = square if total is None else total + square
+            pieces.append((piece * gain_ref[:, chunk * LANES : (chunk + 1) * LANES]).astype(bf16))
+        return jnp.concatenate(pieces, axis=1), jnp.sum(total, axis=1, keepdims=True)
+
+    def parts_copy(phase, peer, slot):
+        return pltpu.make_async_remote_copy(
+            src_ref=parts_out.at[phase, tile_of(peer)],
+            dst_ref=parts_in.at[phase, tile_of(slot)],
+            send_sem=parts_send.at[phase, peer],
+            recv_sem=parts_recv.at[phase, slot],
+            device_id=(peer, req // HALF),
+            device_id_type=MESH,
+        )
+
+    my_slot = ch * HALF + req % HALF
+
+    def is_self(peer):
+        return jnp.logical_and(peer == req, req // HALF == ch)
+
+    def scatter(phase, rows):
+        for index, piece in enumerate(rows):
+            parts_out[phase, pl.ds(index, REQ, stride=TILE), :] = piece
+
+        def start(step, carry):
+            peer = (req + step) % REQ
+
+            @pl.when(jnp.logical_not(is_self(peer)))
+            def _():
+                parts_copy(phase, peer, my_slot).start()
+
+            return carry
+
+        lax.fori_loop(0, REQ, start, 0)
+
+        @pl.when(req // HALF == ch)
+        def _():
+            parts_in[phase, tile_of(my_slot), :] = parts_out[phase, tile_of(req), :]
+
+    def scatter_wait(phase):
+        def wait(slot, carry):
+            mine = jnp.logical_and(slot == my_slot, req // HALF == ch)
+
+            @pl.when(jnp.logical_not(mine))
+            def _():
+                parts_copy(phase, req, slot).wait_recv()
+
+            return carry
+
+        lax.fori_loop(0, CH * HALF, wait, 0)
+
+    def summed(phase, index):
+        pieces = parts_in[phase, pl.ds(index, CH * HALF, stride=TILE), :]
+        return pieces[:HALF] + pieces[HALF:]
+
+    gather(0, own_block[...].astype(bf16))
+    loads[0].wait()
+    loads[1].wait()
+    gather_wait(0)
+    lhs, squares = gained(0, attn_gain_ref)
+    query_part = jnp.dot(lhs, w_query[...], preferred_element_type=f32)
+    keyval_part = jnp.dot(lhs, w_keyval[...], preferred_element_type=f32)
+    per_row = LANES // keyval_part.shape[1]
+    lane = lax.broadcasted_iota(jnp.int32, (ROWS * REQ, LANES), 1)
+    keyval_part = jnp.where(
+        lane // keyval_part.shape[1] == req % per_row,
+        jnp.concatenate([keyval_part] * per_row, axis=1),
+        0.0,
+    )
+    squares = jnp.broadcast_to(squares, (ROWS * REQ, LANES))
+
+    def by_row(array):
+        return [array[row * REQ : (row + 1) * REQ] for row in range(ROWS)]
+
+    scatter(
+        0,
+        by_row(query_part[:, :LANES])
+        + by_row(query_part[:, LANES:])
+        + by_row(keyval_part)
+        + by_row(squares),
+    )
+    loads[2].wait()
+    scatter_wait(0)
+
+    def score_copy(row):
+        return pltpu.make_async_remote_copy(
+            src_ref=score_out.at[row],
+            dst_ref=score_in.at[row],
+            send_sem=score_send.at[row],
+            recv_sem=score_recv.at[row],
+            device_id=(req, other),
+            device_id_type=MESH,
+        )
+
+    own_copy = pltpu.make_async_remote_copy(
+        src_ref=own_out,
+        dst_ref=own_in,
+        send_sem=own_send.at[0],
+        recv_sem=own_recv.at[0],
+        device_id=(req, other),
+        device_id_type=MESH,
+    )
+    values_new = []
+    for row in range(ROWS):
+        scale = lax.rsqrt(summed(0, 6 + row)[:1, :] / D + EPSILON)
+        query = (jnp.concatenate([summed(0, row), summed(0, 2 + row)], axis=0) * scale).astype(bf16)
+        score_out[row] = jnp.dot(query, keys[row], preferred_element_type=f32)
+        score_copy(row).start()
+        keyval = summed(0, 4 + row) * scale
+        key_new = jnp.sum(keyval[: HALF // 2], axis=0, keepdims=True).astype(bf16)
+        value_new = jnp.sum(keyval[HALF // 2 :], axis=0, keepdims=True).astype(bf16)
+        own = jnp.sum(query.astype(f32) * key_new.astype(f32), axis=1, keepdims=True)
+        own_out[row] = jnp.broadcast_to(own, (H, LANES))
+        values_new.append(value_new.astype(f32))
+        result[row : row + 1, :LANES] = key_new.astype(f32)
+        result[row : row + 1, LANES : 2 * LANES] = value_new.astype(f32)
+    own_copy.start()
+    kv_ref[...] = result[:, : 2 * LANES].astype(bf16)
+    loads[3].wait()
+    mixed = []
+    slot_index = lax.broadcasted_iota(jnp.int32, (H, window), 1)
+    for row in range(ROWS):
+        score_copy(row).wait_recv()
+        if row == 0:
+            own_copy.wait_recv()
+        offset = write_pos_ref[row] - 1 - slot_index
+        offset = jnp.where(offset < 0, offset + window, offset)
+        scores = jnp.where(
+            offset < lengths_ref[row], (score_out[row] + score_in[row]) * factor, -jnp.inf
+        )
+        own = (own_out[row] + own_in[row])[:, :1] * factor
+        top = jnp.maximum(jnp.max(scores, axis=1, keepdims=True), own)
+        weights = jnp.exp(scores - top)
+        own_weight = jnp.exp(own - top)
+        total = jnp.sum(weights, axis=1, keepdims=True) + own_weight
+        numer = lax.dot_general(
+            weights.astype(bf16), values[row], (((1,), (1,)), ((), ())), preferred_element_type=f32
+        )
+        numer = numer + own_weight.astype(bf16).astype(f32) * values_new[row]
+        mixed.append(numer / total)
+
+    gather(1, jnp.concatenate(mixed, axis=0).astype(bf16))
+    loads[4].wait()
+    gather_wait(1)
+    lhs = jnp.concatenate([chunk_rows(1, chunk) for chunk in range(CHUNKS)], axis=1).astype(bf16)
+    out_part = jnp.dot(lhs, w_out[...], preferred_element_type=f32)
+    scatter(1, by_row(out_part[:, :LANES]) + by_row(out_part[:, LANES:]))
+    scatter_wait(1)
+    first = jnp.concatenate(
+        [piece for row in range(ROWS) for piece in (summed(1, row), summed(1, 2 + row))], axis=0
+    )
+    first = (own_block[...] + first).astype(bf16)
+    own_block[...] = first.astype(f32)
+
+    gather(2, first)
+    loads[5].wait()
+    loads[6].wait()
+    gather_wait(2)
+    lhs, squares = gained(2, mlp_gain_ref)
+    square_out[...] = jnp.broadcast_to(squares, (ROWS * REQ, LANES))
+    square_copy = pltpu.make_async_remote_copy(
+        src_ref=square_out,
+        dst_ref=square_in,
+        send_sem=square_send.at[0],
+        recv_sem=square_recv.at[0],
+        device_id=(req, other),
+        device_id_type=MESH,
+    )
+    square_copy.start()
+    pieces, _, double = ffn_own.shape
+    width = double // 2
+
+    def ffn_copy(piece):
+        return pltpu.make_async_remote_copy(
+            src_ref=ffn_out.at[piece],
+            dst_ref=ffn_in.at[piece],
+            send_sem=ffn_send.at[piece],
+            recv_sem=ffn_recv.at[piece],
+            device_id=(req, other),
+            device_id_type=MESH,
+        )
+
+    for piece in range(pieces):
+        for part in range(2):
+            begin = part * hidden_cols + piece * width
+            block = jnp.dot(lhs, w_gate_up[:, begin : begin + width], preferred_element_type=f32)
+            ffn_own[piece, :, part * width : (part + 1) * width] = block
+            ffn_out[piece, :, part * width : (part + 1) * width] = block.astype(bf16)
+        ffn_copy(piece).start()
+    square_copy.wait_recv()
+    scale = lax.rsqrt((square_out[...] + square_in[...])[:, :1] / D + EPSILON)
+    hidden = []
+    for piece in range(pieces):
+        ffn_copy(piece).wait_recv()
+        both = (ffn_own[piece] + ffn_in[piece].astype(f32)) * scale
+        hidden.append(
+            (jax.nn.gelu(both[:, :width], approximate=True) * both[:, width:]).astype(bf16)
+        )
+    hidden = jnp.concatenate(hidden, axis=1)
+
+    down = jnp.dot(hidden, w_down[...], preferred_element_type=f32)
+    for chunk in range(CHUNKS):
+        columns = down[:, chunk * LANES : (chunk + 1) * LANES]
+        for row in range(ROWS):
+            down_wide[pl.ds(row * CHUNKS + place(chunk), REQ, stride=BLOCK), :] = columns[
+                row * REQ : (row + 1) * REQ
+            ]
+    down_out[...] = down_wide[...].astype(bf16)
+
+    def down_copy(peer, slot):
+        return pltpu.make_async_remote_copy(
+            src_ref=down_out.at[block_of(peer)],
+            dst_ref=down_in.at[block_of(slot)],
+            send_sem=down_send.at[peer],
+            recv_sem=down_recv.at[slot],
+            device_id=(peer, ch),
+            device_id_type=MESH,
+        )
+
+    def down_start(step, carry):
+        peer = (req + step) % REQ
+        down_copy(peer, req).start()
+        return carry
+
+    lax.fori_loop(1, REQ, down_start, 0)
+    down_in[block_of(req), :] = down_out[block_of(req), :]
+
+    def down_wait(step, carry):
+        peer = (req + REQ - step) % REQ
+        down_copy(peer, peer).wait_recv()
+        return carry
+
+    lax.fori_loop(1, REQ, down_wait, 0)
+    total = down_in[:BLOCK, :].astype(f32)
+    for index in range(1, REQ):
+        total = total + down_in[index * BLOCK : (index + 1) * BLOCK, :].astype(f32)
+    total = total + own_block[...]
+    for row in range(ROWS):
+        for chunk in range(CHUNKS):
+            spot = row * CHUNKS + place(chunk)
+            result[row : row + 1, chunk * LANES : (chunk + 1) * LANES] = total[spot : spot + 1]
+    out_ref[...] = result[...].astype(bf16)
+
+    def drain(step, carry):
+        peer = (req + step) % REQ
+        for phase in range(3):
+            gather_copy(phase, peer, req).wait_send()
+        down_copy(peer, req).wait_send()
+        return carry
+
+    lax.fori_loop(1, REQ, drain, 0)
+
+    def drain_parts(peer, carry):
+        @pl.when(jnp.logical_not(is_self(peer)))
+        def _():
+            for phase in range(2):
+                parts_copy(phase, peer, my_slot).wait_send()
+
+        return carry
+
+    lax.fori_loop(0, REQ, drain_parts, 0)
+    for row in range(ROWS):
+        score_copy(row).wait_send()
+    own_copy.wait_send()
+    square_copy.wait_send()
+    for piece in range(pieces):
+        ffn_copy(piece).wait_send()
+
+
+def fused(
+    tokens,
+    attn_gain,
+    w_query,
+    w_keyval,
+    cache,
+    lengths,
+    write_pos,
+    w_out,
+    mlp_gain,
+    w_gate_up,
+    w_down,
+):
+    f32 = jnp.float32
+    bf16 = jnp.bfloat16
+    window = cache.shape[3]
+    pieces = w_down.shape[0] // 256
+    every = ROWS * REQ
+    vmem = pl.BlockSpec(memory_space=pltpu.VMEM)
+    smem = pl.BlockSpec(memory_space=pltpu.SMEM)
+    hbm = pl.BlockSpec(memory_space=pl.ANY)
+    dma = pltpu.SemaphoreType.DMA
+    return pl.pallas_call(
+        fused_kernel,
+        out_shape=(
+            jax.ShapeDtypeStruct(tokens.shape, bf16),
+            jax.ShapeDtypeStruct((ROWS, 2 * LANES), bf16),
+        ),
+        in_specs=[vmem, vmem, hbm, hbm, hbm, smem, smem, hbm, vmem, hbm, hbm],
+        out_specs=(vmem, vmem),
+        scratch_shapes=[
+            pltpu.VMEM(w_query.shape, bf16),
+            pltpu.VMEM(w_keyval.shape, bf16),
+            pltpu.VMEM(cache.shape[1:], bf16),
+            pltpu.VMEM(cache.shape[1:], bf16),
+            pltpu.VMEM(w_out.shape, bf16),
+            pltpu.VMEM(w_gate_up.shape, bf16),
+            pltpu.VMEM(w_down.shape, bf16),
+            pltpu.VMEM((BLOCK, LANES), f32),
+            pltpu.VMEM((3, BLOCK, LANES), bf16),
+            pltpu.VMEM((3, REQ * BLOCK, LANES), bf16),
+            pltpu.VMEM((3, REQ * BLOCK, LANES), f32),
+            pltpu.VMEM((2, REQ * TILE, LANES), f32),
+            pltpu.VMEM((2, CH * HALF * TILE, LANES), f32),
+            pltpu.VMEM((ROWS, H, window), f32),
+            pltpu.VMEM((ROWS, H, window), f32),
+            pltpu.VMEM((ROWS, H, LANES), f32),
+            pltpu.VMEM((ROWS, H, LANES), f32),
+            pltpu.VMEM((every, LANES), f32),
+            pltpu.VMEM((every, LANES), f32),
+            pltpu.VMEM((pieces, every, 512), f32),
+            pltpu.VMEM((pieces, every, 512), bf16),
+            pltpu.VMEM((pieces, every, 512), bf16),
+            pltpu.VMEM((REQ * BLOCK, LANES), f32),
+            pltpu.VMEM((REQ * BLOCK, LANES), bf16),
+            pltpu.VMEM((REQ * BLOCK, LANES), bf16),
+            pltpu.VMEM(tokens.shape, f32),
+            dma((7,)),
+            dma((3, REQ)),
+            dma((3, REQ)),
+            dma((2, REQ)),
+            dma((2, CH * HALF)),
+            dma((ROWS,)),
+            dma((ROWS,)),
+            dma((1,)),
+            dma((1,)),
+            dma((1,)),
+            dma((1,)),
+            dma((pieces,)),
+            dma((pieces,)),
+            dma((REQ,)),
+            dma((REQ,)),
+        ],
+        compiler_params=pltpu.CompilerParams(
+            collective_id=0, has_side_effects=True, vmem_limit_bytes=48 * 1024 * 1024
+        ),
+    )(
+        tokens,
+        attn_gain.reshape(1, -1),
+        w_query,
+        w_keyval,
+        cache,
+        lengths,
+        write_pos,
+        w_out,
+        mlp_gain.reshape(1, -1),
+        w_gate_up,
+        w_down,
+    )
+
+
 def solution(mesh):
     placed = (
         P("req", "ch"),
@@ -127,8 +652,19 @@
         P("ch", "req"),
         P("req", "ch"),
     )
+    def step(*args):
+        tokens, cache = args[0], args[4]
+        fits = (
+            mesh.shape["ch"] == CH
+            and mesh.shape["req"] == REQ
+            and tokens.shape[0] == ROWS
+            and tokens.shape[1] == CHUNKS * LANES
+            and cache.shape[2] == LANES
+        )
+        return (fused if fits else body)(*args)
+
     return jax.shard_map(
-        body,
+        step,
         mesh=mesh,
         in_specs=placed,
         out_specs=(P("req", "ch"), P("req", "ch")),

time: 352 us -> 65.5 us (0.19)
  waiting for transfers between devices: 206 us -> 0 us
  blocking collectives: 90.3 us -> 0 us
  Pallas kernels: 0 us -> 54.4 us
  between operations: 14.9 us -> 0.66 us
  matrix products: 14 us -> 0 us
  starting transfers between devices: 7.71 us -> 0 us
  other arithmetic: 5.9 us -> 0 us
    unnamed x10 -> x0, waiting for transfers between devices: 159 us -> none
    all_gather x3 -> x0, blocking collectives: 69.8 us -> none  [the longest x1 23.9 us: body(): lax.all_gather(normed, 'req', axis=0, tiled=True)]
    pallas_call x0 -> x1, Pallas kernels: none -> 54.4 us  [fused(): pl.pallas_call(fused_kernel, out_shape=(jax.ShapeDtypeStruct(tokens.shape...]
    psum x2 -> x0, waiting for transfers between devices: 36.8 us -> none  [the longest x1 19 us: body(): summed, own_sum = lax.psum((score_part, own_part), 'ch')]
    dot_general x6 -> x0, matrix products: 14 us -> none  [the longest x1 4.6 us: body(): jnp.dot(lax.all_gather(normed_two, 'req', axis=0, tiled=True), w_gate_up,...]
    psum x3 -> x0, blocking collectives: 11.9 us -> none  [the longest x2 8.16 us: rms_norm(): summed = lax.psum(squares, 'ch')]
    all_to_all x2 -> x0, waiting for transfers between devices: 10.3 us -> none  [the longest x1 5.29 us: body(): lax.all_to_all(head_parts[:, query_cols:], 'req', split_axis=0, concat_ax...]
    all_to_all x1 -> x0, blocking collectives: 8.55 us -> none  [body(): lax.all_to_all(out_parts, 'req', split_axis=0, concat_axis=1, tiled=True)]
  transfers between devices with their start and end apart: 8 -> 0, of which waited for: 8 -> 0; matrix products, arithmetic and copies ran while one was open for 1% -> 0% of each run, Pallas kernels for 0% -> 0%
where the time goes in v1:
time: 65.5 us; the launch traced here: 64.8 us
  Pallas kernels  54.4 us (83%)
  local copies, waits for them, and re-layouts  9.77 us (15%)
  between operations  0.66 us (1%)
    pallas_call x1, Pallas kernels, fused(): pl.pallas_call(fused_kernel, out_shape=(jax.ShapeDtypeStruct(tokens.shape...  54.4 us
    unnamed x19, local copies, waits for them, and re-layouts  9.77 us

profile of v1, /device:TPU:1, one launch (start us, length us, event | category | flops | bytes accessed | tf_op | source)
XLA Modules:
  0.0 64.8 jit_solution(11759256136786637162)
XLA Ops:
  0.6 1.2 %copy.13.w_keyval_hbm = bf16[2048,32]{1,0:T(8,128)(2,1)S(1)} copy(bf16[2048,32]{0,1:T(8,128)(2,1)} %param.14) | data formatting | bytes 262144 | tf_op args[3]
  1.8 0.0 copy-start
  1.8 1.6 %copy-done = bf16[2,2,128,2048]{3,2,1,0:T(8,128)(2,1)S(1)} copy-done((bf16[2,2,128,2048]{3,2,1,0:T(8,128)(2,1)S(1)}, bf16[2,2,128,2048]{3,2,1,0:T(8,128)(2,1)}, u32[]{:S(2)}) %copy-start) | copy-done | bytes 2097176
  3.4 0.0 copy-start.1
  3.4 1.2 %copy-done.1 = bf16[2048,256]{1,0:T(8,128)(2,1)S(1)} copy-done((bf16[2048,256]{1,0:T(8,128)(2,1)S(1)}, bf16[2048,256]{1,0:T(8,128)(2,1)}, u32[]{:S(2)}) %copy-start.1) | copy-done | bytes 1048600
  4.6 0.0 copy-start.2
  4.6 1.2 %copy-done.2 = bf16[2048,256]{1,0:T(8,128)(2,1)S(1)} copy-done((bf16[2048,256]{1,0:T(8,128)(2,1)S(1)}, bf16[2048,256]{1,0:T(8,128)(2,1)}, u32[]{:S(2)}) %copy-start.2) | copy-done | bytes 1048600
  5.9 0.0 copy-start.3
  5.9 0.7 %copy-done.3 = bf16[2,2048]{1,0:T(2,128)(2,1)S(1)} copy-done((bf16[2,2048]{1,0:T(2,128)(2,1)S(1)}, bf16[2,2048]{1,0:T(2,128)(2,1)}, u32[]{:S(2)}) %copy-start.3) | copy-done | bytes 8216
  6.6 0.0 copy-start.4
  6.6 0.7 %copy-done.4 = f32[2048]{0:T(1024)S(1)} copy-done((f32[2048]{0:T(1024)S(1)}, f32[2048]{0:T(1024)}, u32[]{:S(2)}) %copy-start.4) | copy-done | bytes 8216
  7.3 0.0 copy-start.5
  7.3 0.7 %copy-done.5 = f32[2048]{0:T(1024)S(1)} copy-done((f32[2048]{0:T(1024)S(1)}, f32[2048]{0:T(1024)}, u32[]{:S(2)}) %copy-start.5) | copy-done | bytes 8216
  8.0 0.0 copy-start.6
  8.0 0.7 %copy-done.6 = s32[2]{0:T(128)S(1)} copy-done((s32[2]{0:T(128)S(1)}, s32[2]{0:T(128)}, u32[]{:S(2)}) %copy-start.6) | copy-done | bytes 32
  8.6 0.0 copy-start.7
  8.6 0.7 %copy-done.7 = s32[2]{0:T(128)S(1)} copy-done((s32[2]{0:T(128)S(1)}, s32[2]{0:T(128)}, u32[]{:S(2)}) %copy-start.7) | copy-done | bytes 32
  9.3 54.4 %shard_map.122 = (bf16[2,2048]{1,0:T(2,128)(2,1)S(1)}, bf16[2,256]{1,0:T(2,128)(2,1)S(1)}) custom-call(bf16[2,2048]{1,0:T(2,128)(2,1)S(1)} %copy-done.3, f32[1,2048]{1,0:T(1,128)S(1)} %bitcast.2, bf16[2048,256]{1,0:T(8,128)(2,1)S(1)} %copy-done.1, bf16[2048,32]{1,0:T(8,128)(2,1)S(1)} %copy.13.w_keyval_hbm, bf16[2,2,128,2048]{3,2,1,0:T(8,128)(2,1)S(1)} %copy-done, ...), custom_call_target="tpu_custom_call" | custom-call | tf_op jit(solution)/shard_map/pallas_call | solution.py:572
  63.6 0.6 copy.16
  64.2 0.6 copy.17
Async XLA Ops:
  1.8 1.6 %copy-start = (bf16[2,2,128,2048]{3,2,1,0:T(8,128)(2,1)S(1)}, bf16[2,2,128,2048]{3,2,1,0:T(8,128)(2,1)}, u32[]{:S(2)}) copy-start(bf16[2,2,128,2048]{3,2,1,0:T(8,128)(2,1)} %cache_hbm.1) | copy-start | bytes 6291460
  3.4 1.2 %copy-start.1 = (bf16[2048,256]{1,0:T(8,128)(2,1)S(1)}, bf16[2048,256]{1,0:T(8,128)(2,1)}, u32[]{:S(2)}) copy-start(bf16[2048,256]{1,0:T(8,128)(2,1)} %w_query_hbm.1) | copy-start | bytes 3145732
  4.6 1.2 %copy-start.2 = (bf16[2048,256]{1,0:T(8,128)(2,1)S(1)}, bf16[2048,256]{1,0:T(8,128)(2,1)}, u32[]{:S(2)}) copy-start(bf16[2048,256]{1,0:T(8,128)(2,1)} %w_out_hbm.1) | copy-start | bytes 3145732
  5.9 0.7 %copy-start.3 = (bf16[2,2048]{1,0:T(2,128)(2,1)S(1)}, bf16[2,2048]{1,0:T(2,128)(2,1)}, u32[]{:S(2)}) copy-start(bf16[2,2048]{1,0:T(2,128)(2,1)} %tokens_ref.1) | copy-start | bytes 24580
  6.6 0.7 %copy-start.4 = (f32[2048]{0:T(1024)S(1)}, f32[2048]{0:T(1024)}, u32[]{:S(2)}) copy-start(f32[2048]{0:T(1024)} %param.12) | copy-start | bytes 24580
  7.3 0.7 %copy-start.5 = (f32[2048]{0:T(1024)S(1)}, f32[2048]{0:T(1024)}, u32[]{:S(2)}) copy-start(f32[2048]{0:T(1024)} %param.19) | copy-start | bytes 24580
  8.0 0.7 %copy-start.6 = (s32[2]{0:T(128)S(1)}, s32[2]{0:T(128)}, u32[]{:S(2)}) copy-start(s32[2]{0:T(128)} %lengths_ref.1) | copy-start | bytes 28
  8.6 0.7 %copy-start.7 = (s32[2]{0:T(128)S(1)}, s32[2]{0:T(128)}, u32[]{:S(2)}) copy-start(s32[2]{0:T(128)} %write_pos_ref.1) | copy-start | bytes 28
